TPU v7x, 256 devices: a whole 4x4x8 slice. The times are simulated.
256 devices in a mesh: brick: 16 (over y_lo, z), depth: 16 (over x, y_hi, core).
Axes of the slice: x: 4, y: 4 (y_hi: 2, y_lo: 2; y = y_hi * 2 + y_lo), z: 8, core: 2. Of those that a mesh axis runs over, the one named last changes fastest.
Arguments:
- conductivity: float32 [128, 256, 256], P('brick', 'depth'), may hold values from 0.03 to 10.5, as said below
- initial_field: float32 [2, 128, 256, 256], P(None, 'brick', 'depth'), may hold values from -1.2 to 1.2
- adjoint_initial: float32 [2, 128, 256, 256], P(None, 'brick', 'depth'), may hold values from -0.36 to 0.36
- src_cell: int32 [16, 16, 64], P('brick', 'depth'), may hold values from 0 to 32767
- src_amp: float32 [16, 16, 2, 64], P('brick', 'depth'), may hold values from -24 to 24
- rec_cell: int32 [16, 16, 64], P('brick', 'depth'), may hold values from 0 to 32767
- observed: float32 [16, 16, 2, 64], P('brick', 'depth'), may hold values from -12 to 12
- cov_blocks: bfloat16 [16, 16, 16, 512, 512], P('brick', 'depth'), may hold values from -0.25 to 0.25
- cov_rows: int32 [16, 16, 16], P('brick', 'depth'), may hold values from 0 to 63
- cov_cols: int32 [16, 16, 16], P('brick', 'depth'), may hold values from 0 to 1023
Outputs:
- forward: float32 [2, 128, 256, 256], P(None, 'brick', 'depth')
- preconditioned: float32 [128, 256, 256], P('brick', 'depth')
Inputs may be any that keep to these rules, and one draw needn't show every extreme that they name: `conductivity`: positive everywhere.
All inputs are finite; a program needn't handle non-finite values.
Results may differ from a plain program's by a relative error of at most 0.0032.
Values may be sent and summed in bfloat16 or wider, within the bound.
A program may use at most 128 MiB of HBM per device.

v0:
```python
import functools

import jax
import jax.numpy as jnp
from jax import lax
from jax.experimental import pallas as pl
from jax.experimental.pallas import tpu as pltpu
from jax.sharding import PartitionSpec as P

LAPLACE_SHIFTS = (0.5, 2.0)
CENTRE = (6.5, 8.0)
ITERS = 3
NB = 16
CX, CZ, NY = 8, 16, 256
HX, HZ = 6, 8
EX, EZ = CX + 2 * HX, CZ + 2 * HZ
NNZ, BLOCK = 16, 512
ROWS = CX * CZ
F32, BF16 = jnp.float32, jnp.bfloat16
MESH = pl.DeviceIdType.MESH
OWN_X, OWN_Z = pl.ds(HX, CX), pl.ds(HZ, CZ)

FACES_X = ((1, 0), (-1, 0))
FACES_Z = ((0, 1), (0, -1))
CORNERS = ((1, 1), (1, -1), (-1, 1), (-1, -1))
AROUND = FACES_X + FACES_Z + CORNERS

STEPS = sorted(
    ((i, j, k, c) for i in range(4) for j in range(4) for k in range(8) for c in range(2)),
    key=lambda s: -(8 * (min(s[0], 4 - s[0]) + min(s[1], 4 - s[1]) + min(s[2], 8 - s[2])) + s[3]))
PLANE = [s for s in STEPS if s[2:] == (0, 0) and s[:2] != (0, 0)]
COLUMN = [s for s in STEPS if s[:2] == (0, 0) and s[2:] != (0, 0)]
LAYERS = [s for s in STEPS if s[2] == 0 and s[1] % 2 == 0 and s != (0, 0, 0, 0)]


def iota(shape, dim):
    return lax.broadcasted_iota(jnp.int32, shape, dim)


def send_x(dx, width, skip=0):
    return pl.ds(HX + CX - skip - width, width) if dx > 0 else pl.ds(HX + skip, width)


def send_z(dz):
    return pl.ds(HZ + CZ - HZ, HZ) if dz > 0 else pl.ds(HZ, HZ)


def land_x(dx, width, skip=0):
    return pl.ds(HX - skip - width, width) if dx > 0 else pl.ds(HX + CX + skip, width)


def land_z(dz):
    return pl.ds(0, HZ) if dz > 0 else pl.ds(HZ + CZ, HZ)


def layer_at(dx, distance, land):
    if land:
        return HX - distance if dx > 0 else HX + CX + distance - 1
    return HX + CX - distance if dx > 0 else HX + distance - 1


def halves(first, second, dz):
    near = (iota((8, 1), 0) >= 4) if dz > 0 else (iota((8, 1), 0) < 4)
    return jnp.where(near, first, pltpu.roll(second, 4, 0))


def pack_face(field, dz):
    slabs = []
    for m in range(CX // 2):
        tiles = [halves(field[f][2 * m], field[f][2 * m + 1], dz) for f in range(2)]
        slabs.append(jnp.concatenate(tiles, axis=0).astype(BF16))
    return slabs


def pack_corner(field, near, zs, dz):
    tiles = [halves(field[f, near[0], zs, :], field[f, near[1], zs, :], dz) for f in range(2)]
    return tiles + [halves(field[0, near[2], zs, :], field[1, near[2], zs, :], dz)]


def cg_coefficients(nu, centre):
    def inner(p, q, shift):
        total = None
        for i, pi in enumerate(p):
            for j, qj in enumerate(q):
                term = pi * qj * nu[i + j + shift]
                total = term if total is None else total + term
        return total

    one = jnp.ones_like(nu[0])
    r, p = [one], [one]
    rr = nu[0]
    x = [jnp.zeros_like(one)] * ITERS
    for it in range(ITERS):
        step = rr / (inner(p, p, 1) + centre * inner(p, p, 0))
        for i, pi in enumerate(p):
            x[i] = x[i] + step * pi
        if it + 1 < ITERS:
            ap = [centre * pi for pi in p] + [jnp.zeros_like(one)]
            for i, pi in enumerate(p):
                ap[i + 1] = ap[i + 1] + pi
            r = r + [jnp.zeros_like(one)]
            r = [ri - step * ai for ri, ai in zip(r, ap)]
            new = inner(r, r, 0)
            beta = new / rr
            p = p + [jnp.zeros_like(one)]
            p = [ri + beta * pi for ri, pi in zip(r, p)]
            rr = new
    return x


def kernel(
    cond_in, x0_in, a0_in, src_in, amp_in, rec_in, obs_in, cov_in, rows_in, cols_in,
    fwd_out, pre_out,
    src_v, amp_v, rec_v, obs_v, rows_v, cols_v, aux, cov, ce, x0e, a0e, mask, srce, obse, cnte, v0, v1, v2, w, fwd, grad, pre, pick_hot,
    sx, rx, sz, rz, sc, rc, ax, bx, az, bz, ac, bc,
    rlist, seen, rseen, rec_hit, rec_y, cols, asum, rsum, psend, precv,
    in_sem, cov_sem, out_sem, list_sem, cols_sem, halo_sem, adj_sem, seen_sem, sum_sem, pick_sem,
):
    b, d = lax.axis_index("brick"), lax.axis_index("depth")

    def at(dx, dz):
        return lax.rem(b + dx + NB, NB), lax.rem(d + dz + NB, NB)

    barrier = pltpu.get_barrier_semaphore()
    for dx, dz in FACES_X + CORNERS:
        pl.semaphore_signal(barrier, inc=1, device_id=at(dx, dz), device_id_type=MESH)

    cx, cy = lax.div(d, 4), 2 * lax.rem(lax.div(d, 2), 2) + lax.div(b, 8)
    cz, core = lax.rem(b, 8), lax.rem(d, 2)

    def beside(step):
        x, y = lax.rem(cx + step[0], 4), lax.rem(cy + step[1], 4)
        return lax.rem(y, 2) * 8 + lax.rem(cz + step[2], 8), x * 4 + lax.div(y, 2) * 2 + lax.rem(core + step[3], 2)

    greeted = LAYERS + [s for s in PLANE if s[1] % 2] + [s for s in COLUMN if s[2]]
    for step in greeted:
        pl.semaphore_signal(barrier, inc=1, device_id=beside(step), device_id_type=MESH)

    loads = [
        pltpu.make_async_copy(x0_in, x0e.at[:, OWN_X, OWN_Z, :], in_sem.at[0]),
        pltpu.make_async_copy(cond_in, ce.at[OWN_X, OWN_Z, :], in_sem.at[1]),
        pltpu.make_async_copy(src_in, src_v, in_sem.at[2]),
        pltpu.make_async_copy(amp_in, amp_v, in_sem.at[3]),
        pltpu.make_async_copy(rec_in, rec_v, in_sem.at[4]),
        pltpu.make_async_copy(obs_in, obs_v, in_sem.at[5]),
        pltpu.make_async_copy(rows_in, rows_v, in_sem.at[6]),
        pltpu.make_async_copy(cols_in, cols_v, in_sem.at[7]),
        pltpu.make_async_copy(a0_in, a0e.at[:, OWN_X, OWN_Z, :], in_sem.at[8]),
    ]
    for load in loads:
        load.start()
    cov_load = pltpu.make_async_copy(cov_in, cov, cov_sem)
    cov_load.start()

    for load in loads[:2]:
        load.wait()
    for i, (dx, _) in enumerate(FACES_X):
        for f in range(2):
            sx[i, pl.ds(4 * f, 4)] = x0e[f, send_x(dx, 4), OWN_Z, :].astype(BF16)
        sx[i, pl.ds(8, 3)] = ce[send_x(dx, 3), OWN_Z, :].astype(BF16)
    for i, (_, dz) in enumerate(FACES_Z):
        zs = send_z(dz)
        for m, slab in enumerate(pack_face([x0e[f, OWN_X, zs, :] for f in range(2)], dz)):
            sz[i, m] = slab
        for m in range(2):
            tiles = [halves(ce[HX + k, zs, :], ce[HX + k + 1, zs, :], dz) for k in (4 * m, 4 * m + 2)]
            sz[i, 4 + m] = jnp.concatenate(tiles, axis=0).astype(BF16)
    for i, (dx, dz) in enumerate(CORNERS):
        zs = send_z(dz)
        near = [layer_at(dx, k, False) for k in (1, 2, 3)]
        tiles = pack_corner(x0e, near, zs, dz)
        tiles.append(halves(ce[near[0], zs, :], ce[near[1], zs, :], dz))
        sc[i, 0] = jnp.concatenate(tiles[:2], axis=0).astype(BF16)
        sc[i, 1] = jnp.concatenate(tiles[2:], axis=0).astype(BF16)

    for load in loads[2:8]:
        load.wait()

    def twice(row):
        return jnp.concatenate([row, row], axis=1)

    src_cell, rec_cell = src_v[0], rec_v[0]
    aux[0:1, :] = twice((src_cell >> 8).astype(F32))
    aux[1:2, :] = twice((src_cell & (NY - 1)).astype(F32))
    aux[2:4, :] = twice(amp_v[0, 0])
    aux[4:5, :] = twice((rec_cell >> 8).astype(F32))
    aux[5:6, :] = twice((rec_cell & (NY - 1)).astype(F32))
    aux[6:7, :] = jnp.where(iota((1, 128), 1) < 64, 1.0, 0.0)
    aux[7:9, :] = twice(obs_v[0, 0])
    aux[9:16, :] = jnp.zeros((7, 128), F32)
    col_row = jnp.where(iota((NNZ, NNZ), 0) == iota((NNZ, NNZ), 1), cols_v[0].astype(F32), 0.0)
    aux[16:32, :] = jnp.broadcast_to(jnp.sum(col_row, axis=1, keepdims=True), (NNZ, 128))

    pl.semaphore_wait(barrier, len(FACES_X) + len(CORNERS) + len(greeted))

    for n, (dx, dz) in enumerate(AROUND):
        pltpu.make_async_remote_copy(
            src_ref=aux.at[pl.ds(0, 16)], dst_ref=rlist.at[n], send_sem=list_sem.at[0], recv_sem=list_sem.at[1],
            device_id=at(dx, dz), device_id_type=MESH).start()

    def exchange(n, dx, dz, src, dst, sems):
        return pltpu.make_async_remote_copy(
            src_ref=src, dst_ref=dst, send_sem=sems.at[n, 0], recv_sem=sems.at[n, 1],
            device_id=at(dx, dz), device_id_type=MESH)

    halos = []
    for group, s, r in ((FACES_X, sx, rx), (FACES_Z, sz, rz), (CORNERS, sc, rc)):
        for i, (dx, dz) in enumerate(group):
            halos.append(exchange(len(halos), dx, dz, s.at[i], r.at[i], halo_sem))
    for copy in reversed(halos):
        copy.start()

    def inside(dx, dz):
        bx_, dz_ = b + dx, d + dz
        ok = (bx_ >= 0) & (bx_ < NB) & (dz_ >= 0) & (dz_ < NB)
        return jnp.where(ok, 1.0, 0.0).astype(F32)

    for i, (dx, dz) in enumerate(((0, 0),) + AROUND):
        xs = pl.ds(HX, CX) if dx == 0 else land_x(-dx, HX)
        zs = pl.ds(HZ, CZ) if dz == 0 else land_z(-dz)
        nx, nz = (CX if dx == 0 else HX), (CZ if dz == 0 else HZ)
        mask[xs, zs, :] = jnp.full((nx, nz, NY), inside(dx, dz), F32)

    for zs in (pl.ds(0, HZ), pl.ds(HZ + CZ, HZ)):
        for xs in (pl.ds(0, 3), pl.ds(EX - 3, 3)):
            x0e[:, xs, zs, :] = jnp.zeros((2, 3, HZ, NY), F32)
            a0e[:, xs, zs, :] = jnp.zeros((2, 3, HZ, NY), F32)
        for xs in (pl.ds(0, 4), pl.ds(EX - 4, 4)):
            ce[xs, zs, :] = jnp.zeros((4, HZ, NY), F32)

    lane = iota((1, 128), 1)

    def parts(row, ok):
        value = row * ok
        head = value.astype(BF16).astype(F32)
        return jnp.where(lane < 64, head, value - head)

    def where_points(table, base, dx, dz, width):
        xs = pl.ds(HX, CX) if dx == 0 else land_x(-dx, width)
        zs = pl.ds(HZ, CZ) if dz == 0 else land_z(-dz)
        nx, x_low = (CX, 0) if dx == 0 else ((width, 0) if dx > 0 else (width, CX - width))
        nz, z_low = (CZ, 0) if dz == 0 else ((HZ, 0) if dz > 0 else (HZ, CZ - HZ))
        shape = (nx, nz, 128)
        cell_row = ((iota(shape, 0) + x_low) * CZ + iota(shape, 1) + z_low).reshape(nx * nz, 128).astype(F32)
        hit = cell_row == table[base:base + 1, :]
        along_y = (iota((NY, 128), 0).astype(F32) == table[base + 1:base + 2, :]).astype(F32).astype(BF16)
        return hit, along_y, xs, zs, (nx, nz)

    def place(hit, along_y, rows, shape):
        left = jnp.concatenate([jnp.where(hit, row, 0.0).astype(BF16) for row in rows], axis=0)
        placed = lax.dot_general(left, along_y, (((1,), (1,)), ((), ())), preferred_element_type=F32)
        return placed.reshape((len(rows),) + shape + (NY,))

    def place_sources(table, dx, dz):
        ok = inside(dx, dz)
        hit, along_y, xs, zs, shape = where_points(table, 0, dx, dz, 3)
        srce[:, xs, zs, :] = place(hit, along_y, [parts(table[2 + f:3 + f, :], ok) for f in range(2)], shape)

    def place_own_receivers():
        rows = [own_table[6:7, :]] + [parts(own_table[7 + f:8 + f, :], 1.0) for f in range(2)]
        placed = place(*own_points[:2], rows, own_points[4])
        cnte[...] = placed[0]
        obse[...] = placed[1:3]

    own_table = aux[0:16, :]
    place_sources(own_table, 0, 0)

    loads[8].wait()
    for i, (dx, _) in enumerate(FACES_X):
        for f in range(2):
            ax[i, pl.ds(4 * f, 4)] = a0e[f, send_x(dx, 4), OWN_Z, :].astype(BF16)
    for i, (_, dz) in enumerate(FACES_Z):
        for m, slab in enumerate(pack_face([a0e[f, OWN_X, send_z(dz), :] for f in range(2)], dz)):
            az[i, m] = slab
    for i, (dx, dz) in enumerate(CORNERS):
        tiles = pack_corner(a0e, [layer_at(dx, k, False) for k in (1, 2, 3)], send_z(dz), dz)
        ac[i, 0] = jnp.concatenate(tiles[:2], axis=0).astype(BF16)
        ac[i, 1] = jnp.concatenate([tiles[2], tiles[2]], axis=0).astype(BF16)
    adjoint_halos = []
    for group, s, r in ((FACES_X, ax, bx), (FACES_Z, az, bz), (CORNERS, ac, bc)):
        for i, (dx, dz) in enumerate(group):
            adjoint_halos.append(exchange(len(adjoint_halos), dx, dz, s.at[i], r.at[i], adj_sem))

    lists = pltpu.make_async_remote_copy(
        src_ref=rlist, dst_ref=rlist, send_sem=list_sem.at[0], recv_sem=list_sem.at[1],
        device_id=at(1, 0), device_id_type=MESH)
    lists.wait_recv()
    for n, (dx, dz) in enumerate(AROUND):
        place_sources(rlist[n], -dx, -dz)
    for copy in adjoint_halos:
        copy.start()

    def unpack_face(message, field, zs, ok):
        for m in range(CX // 2):
            slab = message[m].astype(F32) * ok
            for f in range(2):
                tile = slab[8 * f:8 * f + 8]
                field[f, HX + 2 * m, zs, :] = tile
                field[f, HX + 2 * m + 1, zs, :] = pltpu.roll(tile, 4, 0)

    def unpack_corner(message, field, near, zs, ok):
        first, second = message[0].astype(F32) * ok, message[1].astype(F32)
        for f in range(2):
            tile = first[8 * f:8 * f + 8]
            field[f, near[0], zs, :] = tile
            field[f, near[1], zs, :] = pltpu.roll(tile, 4, 0)
        tile = second[0:8] * ok
        field[0, near[2], zs, :] = tile
        field[1, near[2], zs, :] = pltpu.roll(tile, 4, 0)
        return second[8:16]

    for n, (dx, dz) in enumerate(AROUND):
        halos[n].wait_recv()
        ok = inside(-dx, -dz)
        if dz == 0:
            for f in range(2):
                x0e[f, land_x(dx, 4), OWN_Z, :] = rx[n, pl.ds(4 * f, 4)].astype(F32) * ok
            ce[land_x(dx, 3), OWN_Z, :] = rx[n, pl.ds(8, 3)].astype(F32)
        elif dx == 0:
            unpack_face(rz.at[n - 2], x0e, land_z(dz), ok)
            for m in range(2):
                slab = rz[n - 2, 4 + m].astype(F32)
                for k in range(2):
                    tile = slab[8 * k:8 * k + 8]
                    ce[HX + 4 * m + 2 * k, land_z(dz), :] = tile
                    ce[HX + 4 * m + 2 * k + 1, land_z(dz), :] = pltpu.roll(tile, 4, 0)
        else:
            near = [layer_at(dx, k, True) for k in (1, 2, 3)]
            second = unpack_corner(rc.at[n - 4], x0e, near, land_z(dz), ok)
            ce[near[0], land_z(dz), :] = second
            ce[near[1], land_z(dz), :] = pltpu.roll(second, 4, 0)

    lane_row = iota((1, 128), 1)

    def around(ref, f, x):
        c = ref[f, x]
        total = ref[f, x - 1] + ref[f, x + 1]
        total = total + pltpu.roll(c, 1, 0) + pltpu.roll(c, EZ - 1, 0)
        up, down = pltpu.roll(c, 1, 1), pltpu.roll(c, NY - 1, 1)
        low = jnp.where(lane_row == 0, 0.0, up[:, 0:128]) + down[:, 0:128]
        high = up[:, 128:] + jnp.where(lane_row == 127, 0.0, down[:, 128:])
        return c, total + jnp.concatenate([low, high], axis=1)

    def fold(first, second):
        p = first[HZ:HZ + CZ] * second[HZ:HZ + CZ]
        return (p[0:8, 0:128] + p[8:16, 0:128]) + (p[0:8, 128:256] + p[8:16, 128:256])

    def residual_layer(x):
        made = []
        for f in range(2):
            c, total = around(x0e, f, x)
            diag = 6.0 + LAPLACE_SHIFTS[f] * ce[x]
            r = (srce[f, x] - (diag * c - total)) * mask[x]
            v0[f, x] = r
            made.append((r, r))
        return made

    def apply_layer(src, dst):
        def run(x):
            made = []
            for f in range(2):
                c, total = around(src, f, x)
                diag = (6.0 - CENTRE[f]) + LAPLACE_SHIFTS[f] * ce[x]
                new = (diag * c - total) * mask[x]
                if dst is not None:
                    dst[f, x] = new
                made.append((c, new))
            return made
        return run

    def sweep(layer, width, want):
        def outer(t, _):
            layer(HX - 1 - t)
            layer(HX + CX + t)
            return 0

        def summed(t, carry):
            for x in [HX + 8 * t + j for j in range(8)]:
                sums = []
                for c, new in layer(x):
                    for which in want:
                        sums.append(fold(c, new) if which == "cross" else fold(new, new))
                carry = tuple(s + t for s, t in zip(carry, sums))
            return carry

        zero = tuple(jnp.zeros((8, 128), F32) for _ in range(2 * len(want)))
        out = lax.fori_loop(0, CX // 8, summed, zero)
        if width:
            for t in range(width):
                outer(t, 0)
        half = len(want)
        return [(out[i], out[half + i]) for i in range(half)]

    def krylov(widths):
        sums = sweep(apply_layer(v0, v1), widths[0], ("cross", "square"))
        sums += sweep(apply_layer(v1, v2), widths[1], ("cross", "square"))
        sums += sweep(apply_layer(v2, None), 0, ("cross",))
        return sums

    low_lanes = iota((8, 128), 1) < 64
    sub = iota((8, 128), 0)

    def start_sum(stage, value):
        asum[stage] = value
        for i, step in enumerate(PLANE if stage % 2 else COLUMN):
            pltpu.make_async_remote_copy(
                src_ref=asum.at[stage], dst_ref=rsum.at[stage, i],
                send_sem=sum_sem.at[stage, 0], recv_sem=sum_sem.at[stage, 1],
                device_id=beside(step), device_id_type=MESH).start()

    def end_sum(stage):
        everything = pltpu.make_async_remote_copy(
            src_ref=rsum.at[stage], dst_ref=rsum.at[stage],
            send_sem=sum_sem.at[stage, 0], recv_sem=sum_sem.at[stage, 1],
            device_id=at(0, 1), device_id_type=MESH)
        everything.wait_recv()
        return asum[stage] + jnp.sum(rsum[stage], axis=0)

    def pack_sums(sums):
        tile = jnp.zeros((8, 128), F32)
        for k, (s0, s1) in enumerate(sums):
            both = jnp.where(low_lanes, s0 + pltpu.roll(s0, 64, 1), s1 + pltpu.roll(s1, 64, 1))
            tile = jnp.where(sub == k, jnp.sum(both, axis=0, keepdims=True), tile)
        return tile

    def coefficients(tile):
        found = []
        for f in range(2):
            keep = low_lanes if f == 0 else jnp.logical_not(low_lanes)
            column = jnp.sum(jnp.where(keep, tile, 0.0), axis=1, keepdims=True)
            nu = [column[k:k + 1, :] for k in range(2 * ITERS)]
            found.append(cg_coefficients(nu, CENTRE[f]))
        return found

    sums = sweep(residual_layer, 3, ("square",))
    sums += krylov((2, 1))
    start_sum(0, pack_sums(sums))

    for i, step in enumerate(LAYERS):
        pltpu.make_async_remote_copy(
            src_ref=aux.at[pl.ds(16, 16)], dst_ref=cols.at[i], send_sem=cols_sem.at[0], recv_sem=cols_sem.at[1],
            device_id=beside(step), device_id_type=MESH).start()

    own_points = where_points(own_table, 4, 0, 0, 0)
    place_own_receivers()
    here = jnp.where(own_points[0], 1.0, 0.0)
    fields = []
    for ref in (x0e, v0, v1, v2):
        for f in range(2):
            fields.append(ref[f, OWN_X, OWN_Z, :].reshape(ROWS, NY))
    fields = jnp.concatenate(fields, axis=0)
    head = fields.astype(BF16)
    tail = (fields - head.astype(F32)).astype(BF16)
    columns = lax.dot_general(head, own_points[1], (((1,), (0,)), ((), ())), preferred_element_type=F32)
    columns += lax.dot_general(tail, own_points[1], (((1,), (0,)), ((), ())), preferred_element_type=F32)
    for j in range(8):
        row = jnp.sum(columns[ROWS * j:ROWS * (j + 1)] * here, axis=0, keepdims=True)
        seen[j:j + 1, :] = row - own_table[7 + j:8 + j, :] if j < 2 else row
    for n, (dx, dz) in enumerate(AROUND):
        pltpu.make_async_remote_copy(
            src_ref=seen, dst_ref=rseen.at[n], send_sem=seen_sem.at[0], recv_sem=seen_sem.at[1],
            device_id=at(dx, dz), device_id_type=MESH).start()
    point_values = pltpu.make_async_remote_copy(
        src_ref=rseen, dst_ref=rseen, send_sem=seen_sem.at[0], recv_sem=seen_sem.at[1],
        device_id=at(1, 0), device_id_type=MESH)
    around_points = []
    for n, (dx, dz) in enumerate(AROUND):
        hit, along_y, xs, zs, shape = where_points(rlist[n], 4, -dx, -dz, 3)
        rec_y[n] = along_y
        count = shape[0] * shape[1]
        rec_hit[n, pl.ds(0, count)] = jnp.where(hit, 1.0, 0.0)
        around_points.append((xs, zs, shape, count))
    for n, (dx, dz) in enumerate(AROUND):
        adjoint_halos[n].wait_recv()
        ok = inside(-dx, -dz)
        if dz == 0:
            for f in range(2):
                a0e[f, land_x(dx, 4), OWN_Z, :] = bx[n, pl.ds(4 * f, 4)].astype(F32) * ok
        elif dx == 0:
            unpack_face(bz.at[n - 2], a0e, land_z(dz), ok)
        else:
            unpack_corner(bc.at[n - 4], a0e, [layer_at(dx, k, True) for k in (1, 2, 3)], land_z(dz), ok)

    start_sum(1, end_sum(0))

    def adjoint_part(t, _):
        for x in (HX - 3 + 2 * t, HX - 2 + 2 * t):
            for f in range(2):
                c, total = around(a0e, f, x)
                diag = 6.0 + LAPLACE_SHIFTS[f] * ce[x]
                w[f, x] = (diag * c - total) * mask[x]
        return 0

    lax.fori_loop(0, CX // 2 + 3, adjoint_part, 0)

    pltpu.make_async_remote_copy(
        src_ref=cols.at[pl.ds(0, NB - 1)], dst_ref=cols.at[pl.ds(0, NB - 1)],
        send_sem=cols_sem.at[0], recv_sem=cols_sem.at[1],
        device_id=at(0, 1), device_id_type=MESH).wait_recv()
    cols[NB - 1] = aux[16:32, :]
    first_row = (d * ROWS).astype(F32)
    row_lane = iota((NNZ, 128), 1).astype(F32)

    def request(slot, _):
        row = 2.0 * cols[slot] - first_row
        hot = jnp.concatenate([jnp.where(row == row_lane, 1.0, 0.0), jnp.where(row + 1.0 == row_lane, 1.0, 0.0)], axis=0)
        pick_hot[pl.ds(pl.multiple_of(slot * 2 * NNZ, 2 * NNZ), 2 * NNZ)] = hot.astype(BF16)
        return 0

    lax.fori_loop(0, NB, request, 0)

    point_values.wait_recv()
    found = coefficients(end_sum(1))

    for n, (dx, dz) in enumerate(AROUND):
        xs, zs, shape, count = around_points[n]
        ok = inside(-dx, -dz)
        left = []
        for f in range(2):
            a = found[f]
            values = rseen[n, f:f + 1, :]
            for k in range(ITERS):
                values = values + a[k] * rseen[n, 2 * (k + 1) + f:2 * (k + 1) + f + 1, :]
            left.append((rec_hit[n, pl.ds(0, count)] * parts(values, ok)).astype(BF16))
        placed = lax.dot_general(jnp.concatenate(left, axis=0), rec_y[n], (((1,), (1,)), ((), ())),
                                 preferred_element_type=F32).reshape((2,) + shape + (NY,))
        v0[:, xs, zs, :] = placed - w[:, xs, zs, :]

    def own_residual(t, carry):
        for x in [HX + 8 * t + j for j in range(8)]:
            out = []
            for f in range(2):
                a = found[f]
                new = x0e[f, x, OWN_Z, :] + a[0] * v0[f, x, OWN_Z, :] + a[1] * v1[f, x, OWN_Z, :]
                new = new + a[2] * v2[f, x, OWN_Z, :]
                fwd[f, x - HX] = new
                u = cnte[x - HX] * new - obse[f, x - HX] - w[f, x, OWN_Z, :]
                v0[f, x, OWN_Z, :] = u
                p = u * u
                out.append(carry[f] + (p[0:8, 0:128] + p[8:16, 0:128]) + (p[0:8, 128:256] + p[8:16, 128:256]))
            carry = tuple(out)
        return carry

    squares = lax.fori_loop(0, CX // 8, own_residual, (jnp.zeros((8, 128), F32),) * 2)
    forward_store = pltpu.make_async_copy(fwd, fwd_out, out_sem.at[0])
    forward_store.start()

    sums = [squares] + krylov((2, 1))
    start_sum(2, pack_sums(sums))
    start_sum(3, end_sum(2))
    found_adjoint = coefficients(end_sum(3))

    def gradient_layer(x, _):
        total = jnp.zeros((CZ, NY), F32)
        for f in range(2):
            e = found_adjoint[f]
            own = a0e[f, x + HX, OWN_Z, :] + e[0] * v0[f, x + HX, OWN_Z, :] + e[1] * v1[f, x + HX, OWN_Z, :]
            own = own + e[2] * v2[f, x + HX, OWN_Z, :]
            total = total + LAPLACE_SHIFTS[f] * fwd[f, x] * own
        grad[pl.ds(x * CZ, CZ)] = (-total).astype(BF16)
        return 0

    for x in range(CX):
        gradient_layer(x, 0)

    psend[...] = jnp.dot(pick_hot[...], grad[...], preferred_element_type=F32).astype(BF16).reshape(NB, 2 * NNZ, NY)

    for i, step in enumerate(LAYERS):
        back = ((4 - step[0]) % 4,) + step[1:]
        pltpu.make_async_remote_copy(
            src_ref=psend.at[i], dst_ref=precv.at[i], send_sem=pick_sem.at[0], recv_sem=pick_sem.at[1],
            device_id=beside(back), device_id_type=MESH).start()

    cov_load.wait()
    picks = pltpu.make_async_remote_copy(
        src_ref=precv, dst_ref=precv, send_sem=pick_sem.at[0], recv_sem=pick_sem.at[1],
        device_id=at(0, 1), device_id_type=MESH)
    picks.wait_recv()
    picked = psend[NB - 1].astype(F32) + jnp.sum(precv[...].astype(F32), axis=0)
    picked = picked.astype(BF16)

    term_row = iota((NNZ, BLOCK), 0)

    def term(t, total):
        for k in range(NNZ):
            block = cov[k]
            made = lax.dot_general(picked[0:NNZ], block[:, 0:NY], (((1,), (1,)), ((), ())), preferred_element_type=F32)
            made += lax.dot_general(picked[NNZ:], block[:, NY:], (((1,), (1,)), ((), ())), preferred_element_type=F32)
            total = jnp.where(term_row == k, made, total)
        return total

    terms = lax.fori_loop(0, 1, term, jnp.zeros((NNZ, BLOCK), F32))
    cov_rows = rows_v[0].astype(F32)
    out_row = iota((ROWS, NNZ), 0).astype(F32)
    total = grad[...].astype(F32)
    for half in range(2):
        hot = jnp.where(2.0 * cov_rows + float(half) == out_row, 1.0, 0.0)
        total = total + jnp.dot(hot, terms[:, half * NY:(half + 1) * NY], precision=lax.Precision.HIGHEST,
                                preferred_element_type=F32)
    pre[...] = total.reshape(CX, CZ, NY)
    pre_store = pltpu.make_async_copy(pre, pre_out, out_sem.at[1])
    pre_store.start()

    lists.wait_send()
    for copy in halos + adjoint_halos + [point_values]:
        copy.wait_send()
    pltpu.make_async_remote_copy(
        src_ref=cols.at[pl.ds(0, NB - 1)], dst_ref=cols.at[pl.ds(0, NB - 1)],
        send_sem=cols_sem.at[0], recv_sem=cols_sem.at[1],
        device_id=at(0, 1), device_id_type=MESH).wait_send()
    for stage in range(4):
        pltpu.make_async_remote_copy(
            src_ref=rsum.at[stage], dst_ref=rsum.at[stage],
            send_sem=sum_sem.at[stage, 0], recv_sem=sum_sem.at[stage, 1],
            device_id=at(0, 1), device_id_type=MESH).wait_send()
    picks.wait_send()
    forward_store.wait()
    pre_store.wait()


def hand_over(fwd_in, pre_in, fwd_out, pre_out):
    fwd_out[...] = fwd_in[...]
    pre_out[...] = pre_in[...]


def local(conductivity, initial_field, adjoint_initial, src_cell, src_amp, rec_cell, observed, cov_blocks, cov_rows, cov_cols):
    big = pltpu.VMEM((2, EX, EZ, NY), F32)
    one = pltpu.VMEM((EX, EZ, NY), F32)
    dma = pltpu.SemaphoreType.DMA
    scratch = [
        pltpu.VMEM(src_cell.shape, jnp.int32), pltpu.VMEM(src_amp.shape, F32),
        pltpu.VMEM(rec_cell.shape, jnp.int32), pltpu.VMEM(observed.shape, F32),
        pltpu.VMEM(cov_rows.shape, jnp.int32), pltpu.VMEM(cov_cols.shape, jnp.int32),
        pltpu.VMEM((32, 128), F32), pltpu.VMEM((NNZ, BLOCK, BLOCK), BF16),
        one, big, big, one, big,
        pltpu.VMEM((2, CX, CZ, NY), F32), pltpu.VMEM((CX, CZ, NY), F32),
        big, big, big, big,
        pltpu.VMEM((2, CX, CZ, NY), F32), pltpu.VMEM((ROWS, NY), BF16), pltpu.VMEM((CX, CZ, NY), F32),
        pltpu.VMEM((2 * NNZ * NB, ROWS), BF16),
    ]
    for count, slabs in ((2, 11), (2, 6), (4, 2), (2, 8), (2, 4), (4, 2)):
        scratch += [pltpu.VMEM((count, slabs, 16, NY), BF16)] * 2
    scratch += [
        pltpu.VMEM((8, 16, 128), F32), pltpu.VMEM((8, 128), F32), pltpu.VMEM((8, 8, 128), F32),
        pltpu.VMEM((8, 64, 128), F32), pltpu.VMEM((8, NY, 128), BF16), pltpu.VMEM((NB, NNZ, 128), F32),
        pltpu.VMEM((4, 8, 128), F32), pltpu.VMEM((4, NB - 1, 8, 128), F32),
        pltpu.VMEM((NB, 2 * NNZ, NY), BF16), pltpu.VMEM((NB - 1, 2 * NNZ, NY), BF16),
        dma((9,)), dma, dma((2,)), dma((2,)), dma((2,)), dma((8, 2)), dma((8, 2)), dma((2,)), dma((4, 2)), dma((2,)),
    ]
    anywhere = pl.BlockSpec(memory_space=pl.ANY)
    results = pl.pallas_call(
        kernel,
        out_shape=(
            jax.ShapeDtypeStruct((2, CX, CZ, NY), F32),
            jax.ShapeDtypeStruct((CX, CZ, NY), F32),
        ),
        in_specs=[anywhere] * 10,
        out_specs=(anywhere, anywhere),
        scratch_shapes=scratch,
        compiler_params=pltpu.CompilerParams(
            collective_id=0, has_side_effects=True, vmem_limit_bytes=56 * 2**20),
    )(conductivity, initial_field, adjoint_initial, src_cell, src_amp, rec_cell, observed,
      cov_blocks.reshape(NNZ, BLOCK, BLOCK), cov_rows, cov_cols)
    return pl.pallas_call(
        hand_over,
        out_shape=[jax.ShapeDtypeStruct(r.shape, r.dtype) for r in results],
    )(*results)


def solution(mesh):
    return jax.shard_map(
        local,
        mesh=mesh,
        in_specs=(
            P("brick", "depth", None),
            P(None, "brick", "depth", None),
            P(None, "brick", "depth", None),
            P("brick", "depth", None),
            P("brick", "depth", None, None),
            P("brick", "depth", None),
            P("brick", "depth", None, None),
            P("brick", "depth", None, None, None),
            P("brick", "depth", None),
            P("brick", "depth", None),
        ),
        out_specs=(P(None, "brick", "depth", None), P("brick", "depth", None)),
        check_vma=False,
    )
```

profile of v0, /device:TPU:1, one launch (start us, length us, event | category | flops | bytes accessed | tf_op | source)
XLA Modules:
  0.0 51.4 jit_solution(14226277245933606007)
XLA Ops:
  0.6 49.0 %shard_map.113 = (f32[2,8,16,256]{3,2,1,0:T(8,128)}, f32[8,16,256]{2,1,0:T(8,128)}) custom-call(f32[8,16,256]{2,1,0:T(8,128)} %cond_in.1, f32[2,8,16,256]{3,2,1,0:T(8,128)} %x0_in.1, f32[2,8,16,256]{3,2,1,0:T(8,128)} %a0_in.1, s32[1,1,64]{2,1,0:T(1,128)} %src_in.1, f32[1,1,2,64]{3,2,1,0:T(2,128)} %amp_in.1, s32[1,1,64]{2,1,0:T(1,128)} %rec_in.1, ...), custom_call_target="tpu_custom_call" | custom-call | tf_op jit(solution)/shard_map/pallas_call | solution.py:651
  49.6 1.7 %shard_map.114 = (f32[2,8,16,256]{3,2,1,0:T(8,128)}, f32[8,16,256]{2,1,0:T(8,128)}) custom-call(f32[2,8,16,256]{3,2,1,0:T(8,128)} %get-tuple-element.4.fwd_in, f32[8,16,256]{2,1,0:T(8,128)} %get-tuple-element.5.pre_in), custom_call_target="tpu_custom_call" | custom-call | tf_op jit(solution)/shard_map/pallas_call | solution.py:664
where the time goes:
time: 51.5 us; the launch traced here: 51.4 us
  Pallas kernels  50.7 us (98%)
  between operations  0.64 us (1%)
    pallas_call x1, Pallas kernels, local(): pl.pallas_call(kernel, out_shape=(jax.ShapeDtypeStruct((2, CX, CZ, NY), F...  49 us
    pallas_call x1, Pallas kernels, local(): pl.pallas_call(hand_over, out_shape=[jax.ShapeDtypeStruct(r.shape, r.dtyp...  1.74 us

commit v1 on v0

--- a/solution.py
+++ b/solution.py
@@ -111,7 +111,7 @@
 def kernel(
     cond_in, x0_in, a0_in, src_in, amp_in, rec_in, obs_in, cov_in, rows_in, cols_in,
     fwd_out, pre_out,
-    src_v, amp_v, rec_v, obs_v, rows_v, cols_v, aux, cov, ce, x0e, a0e, mask, srce, obse, cnte, v0, v1, v2, w, fwd, grad, pre, pick_hot,
+    src_v, amp_v, rec_v, obs_v, rows_v, cols_v, aux, cov, ce, x0e, a0e, mask, srce, obse, cnte, v0, v1, v2, w, diagonal, fwd, grad, pre, pick_hot,
     sx, rx, sz, rz, sc, rc, ax, bx, az, bz, ac, bc,
     rlist, seen, rseen, rec_hit, rec_y, cols, asum, rsum, psend, precv,
     in_sem, cov_sem, out_sem, list_sem, cols_sem, halo_sem, adj_sem, seen_sem, sum_sem, pick_sem,
@@ -355,13 +355,16 @@
             made.append((r, r))
         return made
 
-    def apply_layer(src, dst):
+    def apply_layer(src, dst, ready=False):
         def run(x):
             made = []
             for f in range(2):
                 c, total = around(src, f, x)
-                diag = (6.0 - CENTRE[f]) + LAPLACE_SHIFTS[f] * ce[x]
-                new = (diag * c - total) * mask[x]
+                if ready:
+                    new = diagonal[f, x] * c - total * mask[x]
+                else:
+                    diag = (6.0 - CENTRE[f]) + LAPLACE_SHIFTS[f] * ce[x]
+                    new = (diag * c - total) * mask[x]
                 if dst is not None:
                     dst[f, x] = new
                 made.append((c, new))
@@ -391,10 +394,10 @@
         half = len(want)
         return [(out[i], out[half + i]) for i in range(half)]
 
-    def krylov(widths):
-        sums = sweep(apply_layer(v0, v1), widths[0], ("cross", "square"))
-        sums += sweep(apply_layer(v1, v2), widths[1], ("cross", "square"))
-        sums += sweep(apply_layer(v2, None), 0, ("cross",))
+    def krylov(widths, ready=False):
+        sums = sweep(apply_layer(v0, v1, ready), widths[0], ("cross", "square"))
+        sums += sweep(apply_layer(v1, v2, ready), widths[1], ("cross", "square"))
+        sums += sweep(apply_layer(v2, None, ready), 0, ("cross",))
         return sums
 
     low_lanes = iota((8, 128), 1) < 64
@@ -489,6 +492,7 @@
                 c, total = around(a0e, f, x)
                 diag = 6.0 + LAPLACE_SHIFTS[f] * ce[x]
                 w[f, x] = (diag * c - total) * mask[x]
+                diagonal[f, x] = (diag - CENTRE[f]) * mask[x]
         return 0
 
     lax.fori_loop(0, CX // 2 + 3, adjoint_part, 0)
@@ -545,7 +549,7 @@
     forward_store = pltpu.make_async_copy(fwd, fwd_out, out_sem.at[0])
     forward_store.start()
 
-    sums = [squares] + krylov((2, 1))
+    sums = [squares] + krylov((2, 1), True)
     start_sum(2, pack_sums(sums))
     start_sum(3, end_sum(2))
     found_adjoint = coefficients(end_sum(3))
@@ -576,8 +580,9 @@
         src_ref=precv, dst_ref=precv, send_sem=pick_sem.at[0], recv_sem=pick_sem.at[1],
         device_id=at(0, 1), device_id_type=MESH)
     picks.wait_recv()
-    picked = psend[NB - 1].astype(F32) + jnp.sum(precv[...].astype(F32), axis=0)
-    picked = picked.astype(BF16)
+    picked = psend[NB - 1]
+    for i in range(NB - 1):
+        picked = picked + precv[i]
 
     term_row = iota((NNZ, BLOCK), 0)
 
@@ -634,7 +639,7 @@
         pltpu.VMEM((32, 128), F32), pltpu.VMEM((NNZ, BLOCK, BLOCK), BF16),
         one, big, big, one, big,
         pltpu.VMEM((2, CX, CZ, NY), F32), pltpu.VMEM((CX, CZ, NY), F32),
-        big, big, big, big,
+        big, big, big, big, big,
         pltpu.VMEM((2, CX, CZ, NY), F32), pltpu.VMEM((ROWS, NY), BF16), pltpu.VMEM((CX, CZ, NY), F32),
         pltpu.VMEM((2 * NNZ * NB, ROWS), BF16),
     ]

time: 51.5 us -> 51.5 us (level)
  no operation moved by 1% of the time
where the time goes in v1:
time: 51.5 us; the launch traced here: 51.4 us
  Pallas kernels  50.7 us (98%)
  between operations  0.64 us (1%)
    pallas_call x1, Pallas kernels, local(): pl.pallas_call(kernel, out_shape=(jax.ShapeDtypeStruct((2, CX, CZ, NY), F...  49 us
    pallas_call x1, Pallas kernels, local(): pl.pallas_call(hand_over, out_shape=[jax.ShapeDtypeStruct(r.shape, r.dtyp...  1.74 us

profile of v1, /device:TPU:1, one launch (start us, length us, event | category | flops | bytes accessed | tf_op | source)
XLA Modules:
  0.0 51.4 jit_solution(10869305265988314149)
XLA Ops:
  0.6 49.0 %shard_map.113 = (f32[2,8,16,256]{3,2,1,0:T(8,128)}, f32[8,16,256]{2,1,0:T(8,128)}) custom-call(f32[8,16,256]{2,1,0:T(8,128)} %cond_in.1, f32[2,8,16,256]{3,2,1,0:T(8,128)} %x0_in.1, f32[2,8,16,256]{3,2,1,0:T(8,128)} %a0_in.1, s32[1,1,64]{2,1,0:T(1,128)} %src_in.1, f32[1,1,2,64]{3,2,1,0:T(2,128)} %amp_in.1, s32[1,1,64]{2,1,0:T(1,128)} %rec_in.1, ...), custom_call_target="tpu_custom_call" | custom-call | tf_op jit(solution)/shard_map/pallas_call | solution.py:656
  49.6 1.7 %shard_map.114 = (f32[2,8,16,256]{3,2,1,0:T(8,128)}, f32[8,16,256]{2,1,0:T(8,128)}) custom-call(f32[2,8,16,256]{3,2,1,0:T(8,128)} %get-tuple-element.4.fwd_in, f32[8,16,256]{2,1,0:T(8,128)} %get-tuple-element.5.pre_in), custom_call_target="tpu_custom_call" | custom-call | tf_op jit(solution)/shard_map/pallas_call | solution.py:669
